TPU v7x, 32 devices: a whole 2x2x4 slice. The times are simulated.
32 devices in a mesh: head: 4 (over z), outer: 2 (over x), inner: 4 (over y, core).
Axes of the slice: x: 2, y: 2, z: 4, core: 2. Of those that a mesh axis runs over, the one named last changes fastest.
Arguments:
- tokens: bfloat16 [4096, 8192], P(('outer', 'inner')), may hold values from -16 to 16
- positions: int32 [4096], replicated, may hold values from 0 to 4095, as said below
- w_query: bfloat16 [8192, 4096], P(None, 'head'), as said below
- w_keyval: bfloat16 [8192, 1024], P(None, 'head'), as said below
Outputs:
- attended: bfloat16 [4096, 4096], P(('outer', 'inner'), 'head')
Inputs may be any that keep to these rules, and one draw needn't show every extreme that they name: positions is a permutation of 0 to 4095 made of runs of 256 consecutive rising positions, each run starting at a multiple of 256. `w_query`: entries are of the order of the inverse square root of 8192. `w_keyval`: entries are of the order of the inverse square root of 8192.
All inputs are finite; a program needn't handle non-finite values.
Results may differ from a plain program's by a relative error of at most 0.011.
Values may be sent and summed in bfloat16 or wider, within the bound.
No kernel may reach another device: no remote copies, remote signals or barrier semaphores. Data moves between devices by JAX's collectives and lax.ppermute only.
A program may use at most 128 MiB of HBM per device.

v0:
```python
import functools
import math

import jax
import jax.numpy as jnp
import numpy as np
from jax import lax
from jax.experimental import pallas as pl
from jax.experimental.pallas import tpu as pltpu
from jax.sharding import PartitionSpec as P

HEAD_DIM = 128
HALF = HEAD_DIM // 2
SPAN = 256
ROPE_BASE = 500000.0
NEG_FILL = -1e30
LOG2_SCALE = math.log2(math.e) / math.sqrt(HEAD_DIM)
MIB = 1024 * 1024
BLOCK = 256
DEPTH = 1024
WINDOW = 3
GROUP = 4
AHEAD = 1
PACK = 4
SEQ_AXES = ("outer", "inner")


def rotation_tables(runs):
    freqs = ROPE_BASE ** (-(np.arange(HALF, dtype=np.float64) * 2.0) / HEAD_DIM)
    freqs = np.concatenate([freqs, freqs])
    within = np.arange(SPAN, dtype=np.float64)[:, None] * freqs
    starts = (np.arange(runs, dtype=np.float64) * SPAN)[:, None] * freqs
    within = np.stack([np.cos(within), np.sin(within)]).astype(np.float32)
    starts = np.stack([np.cos(starts), np.sin(starts)], 1).astype(np.float32)
    return jnp.asarray(within), jnp.asarray(starts)


def run_rotation(within_ref, starts_ref, run):
    cos_in, sin_in = within_ref[0], within_ref[1]
    start = starts_ref[run]
    cos_at, sin_at = start[0:1], start[1:2]
    lane = lax.broadcasted_iota(jnp.int32, (SPAN, HEAD_DIM), 1)
    cosine = cos_in * cos_at - sin_in * sin_at
    sine = sin_in * cos_at + cos_in * sin_at
    return jnp.where(lane < HALF, cosine, sine)


def spread(turn):
    lane = lax.broadcasted_iota(jnp.int32, turn.shape, 1)
    other = pltpu.roll(turn, HALF, 1)
    return jnp.where(lane < HALF, turn, other), jnp.where(lane < HALF, -other, turn)


def rotate(rows, cosine, sine):
    return rows * cosine + pltpu.roll(rows, HALF, 1) * sine


def own_start(pos_ref, index):
    row = lax.axis_index("outer") * lax.axis_size("inner") + lax.axis_index("inner")
    return pos_ref[row * (2 * SPAN) + index * SPAN]


def accumulate(
    depths, tokens_hbm, w_hbm, tokens_ref, w_ref, total, token_sems, w_sems, beside, finish
):
    columns = w_ref.shape[1]
    chunks = len(depths)
    parts = [pl.ds(sum(depths[:chunk]), depths[chunk]) for chunk in range(chunks)]
    copies = [
        (
            pltpu.make_async_copy(
                tokens_hbm.at[:, part], tokens_ref.at[:, part], token_sems.at[chunk]
            ),
            pltpu.make_async_copy(w_hbm.at[part], w_ref.at[part], w_sems.at[chunk]),
        )
        for chunk, part in enumerate(parts)
    ]
    for pair in copies[:WINDOW]:
        for copy in pair:
            copy.start()
    for chunk, (part, pair) in enumerate(zip(parts, copies)):
        for copy in pair:
            copy.wait()
        if chunk + WINDOW < chunks:
            for copy in copies[chunk + WINDOW]:
                copy.start()
        if chunk == 1:
            beside()
        if chunk < chunks - 1:
            product = jnp.dot(
                tokens_ref[:, part], w_ref[part], preferred_element_type=jnp.float32
            )
            total[...] = product if chunk == 0 else total[...] + product
            continue
        for block in range(columns // BLOCK):
            cols = pl.ds(block * BLOCK, BLOCK)
            product = total[:, cols] + jnp.dot(
                tokens_ref[:, part], w_ref[part, cols], preferred_element_type=jnp.float32
            )
            for head in range(BLOCK // HEAD_DIM):
                finish(
                    block * BLOCK + head * HEAD_DIM,
                    product[:, head * HEAD_DIM : (head + 1) * HEAD_DIM],
                )


def keyval_kernel(
    depths, pos_hbm, within_hbm, starts_hbm, tokens_hbm, w_hbm, out_ref, turn_hbm, tokens_ref,
    w_ref, total, turn_ref, turn_sem, token_sems, w_sems, pos_ref, within_ref, starts_ref, table_sems
):
    tables = [
        pltpu.make_async_copy(pos_hbm, pos_ref, table_sems.at[0]),
        pltpu.make_async_copy(within_hbm, within_ref, table_sems.at[1]),
        pltpu.make_async_copy(starts_hbm, starts_ref, table_sems.at[2]),
    ]
    for copy in tables:
        copy.start()
    turn_copy = pltpu.make_async_copy(
        turn_ref, turn_hbm.at[pl.ds(0, turn_ref.shape[0])], turn_sem
    )

    def beside():
        for copy in tables:
            copy.wait()
        for run in range(out_ref.shape[0] // SPAN):
            turn_ref[pl.ds(run * SPAN, SPAN)] = run_rotation(
                within_ref, starts_ref, lax.div(own_start(pos_ref, run), SPAN)
            )
        turn_copy.start()

    def finish(place, piece):
        if place < HEAD_DIM:
            piece = rotate(piece, *spread(turn_ref[...]))
        out_ref[:, place : place + HEAD_DIM] = piece.astype(out_ref.dtype)

    accumulate(
        depths, tokens_hbm, w_hbm, tokens_ref, w_ref, total, token_sems, w_sems, beside, finish
    )
    turn_copy.wait()


def query_kernel(
    depths, turn_hbm, tokens_hbm, w_hbm, out_ref, tokens_ref, w_ref, total, turn_ref, turn_sem,
    token_sems, w_sems
):
    turn_copy = pltpu.make_async_copy(
        turn_hbm.at[pl.ds(0, turn_ref.shape[0])], turn_ref, turn_sem
    )
    turn_copy.start()

    def finish(place, piece):
        piece = rotate(piece, *spread(turn_ref[...]))
        out_ref[:, place : place + HEAD_DIM] = piece.astype(out_ref.dtype)

    accumulate(
        depths, tokens_hbm, w_hbm, tokens_ref, w_ref, total, token_sems, w_sems, turn_copy.wait,
        finish,
    )


def project(kernel, depths, others, tokens, weights, more_out, more_scratch, limit):
    rows, width = tokens.shape
    columns = weights.shape[1]
    vmem = pl.BlockSpec(memory_space=pltpu.VMEM)
    hbm = pl.BlockSpec(memory_space=pltpu.HBM)
    return pl.pallas_call(
        functools.partial(kernel, depths),
        in_specs=[hbm] * (len(others) + 2),
        out_specs=[vmem] + [hbm] * len(more_out),
        out_shape=[jax.ShapeDtypeStruct((rows, columns), jnp.bfloat16)] + more_out,
        scratch_shapes=[
            pltpu.VMEM(tokens.shape, tokens.dtype),
            pltpu.VMEM(weights.shape, weights.dtype),
            pltpu.VMEM((rows, columns), jnp.float32),
            pltpu.VMEM((rows, HEAD_DIM), jnp.float32),
            pltpu.SemaphoreType.DMA,
            pltpu.SemaphoreType.DMA((len(depths),)),
            pltpu.SemaphoreType.DMA((len(depths),)),
        ]
        + more_scratch,
        compiler_params=pltpu.CompilerParams(vmem_limit_bytes=limit * MIB),
        cost_estimate=pl.CostEstimate(
            flops=2 * rows * width * columns,
            bytes_accessed=2 * (rows * width + width * columns),
            transcendentals=0,
        ),
    )(*others, tokens, weights)


def keyval(tokens, w_keyval, positions):
    within, starts = rotation_tables(positions.shape[0] // SPAN)
    return project(
        keyval_kernel,
        (DEPTH,) * (tokens.shape[1] // DEPTH),
        [positions, within, starts],
        tokens,
        w_keyval,
        [jax.ShapeDtypeStruct((tokens.shape[0] * 64, HEAD_DIM), jnp.float32)],
        [
            pltpu.SMEM(positions.shape, positions.dtype),
            pltpu.VMEM(within.shape, within.dtype),
            pltpu.VMEM(starts.shape, starts.dtype),
            pltpu.SemaphoreType.DMA((3,)),
        ],
        58,
    )


def attention_kernel(masks, last, pos_ref, q_ref, kv_ref, *refs):
    if last:
        _, _, out_ref, top_ref, total_ref, order = refs
    else:
        top_ref, total_ref, order = refs
    heads = q_ref.shape[1] // HEAD_DIM
    me = lax.axis_index("outer") * lax.axis_size("inner") + lax.axis_index("inner")
    packs = heads // PACK
    causal = lax.broadcasted_iota(jnp.int32, (SPAN, SPAN), 1) <= lax.broadcasted_iota(
        jnp.int32, (SPAN, SPAN), 0
    )
    causal = jnp.concatenate([causal] * PACK, 0)
    ones = jnp.ones((SPAN, HEAD_DIM), jnp.bfloat16)

    def visit(part, slots, first):
        rows = pl.ds(pl.multiple_of(part * SPAN, SPAN), SPAN)
        starts = [pl.multiple_of(slot * SPAN, SPAN) for slot in slots]
        keys = [kv_ref[pl.ds(start, SPAN), :HEAD_DIM] for start in starts]
        values = jnp.concatenate(
            [
                jnp.concatenate([kv_ref[pl.ds(start, SPAN), HEAD_DIM:], ones], 1)
                for start in starts
            ],
            0,
        )

        def score(pack):
            queries = jnp.concatenate(
                [
                    q_ref[rows, head * HEAD_DIM : (head + 1) * HEAD_DIM]
                    for head in range(pack * PACK, (pack + 1) * PACK)
                ],
                0,
            )
            return [
                lax.dot_general(
                    queries, key, (((1,), (1,)), ((), ())), preferred_element_type=jnp.float32
                )
                for key in keys
            ]

        def weigh(pack, scores):
            if first:
                scores[0] = jnp.where(causal, scores[0], NEG_FILL)
            best = jnp.max(functools.reduce(jnp.maximum, scores), axis=1, keepdims=True)
            if first:
                top, factor = jnp.broadcast_to(best, (PACK * SPAN, HEAD_DIM)), None
            else:
                before = top_ref[part, pack]
                top = jnp.maximum(before, best)
                factor = jnp.exp2((before - top) * LOG2_SCALE)
            top_ref[part, pack] = top
            wide = jnp.concatenate([top, top], 1)
            weights = [
                jnp.exp2((piece - wide) * LOG2_SCALE).astype(jnp.bfloat16) for piece in scores
            ]
            return jnp.concatenate(weights, 1), factor

        def add(pack, weights, factor):
            added = jnp.dot(weights, values, preferred_element_type=jnp.float32)
            if first:
                total_ref[part, pack] = added
            else:
                total_ref[part, pack] = (
                    total_ref[part, pack] * jnp.concatenate([factor, factor], 1) + added
                )

        scores = [score(pack) for pack in range(AHEAD)]
        weighed = None
        for pack in range(packs):
            if pack + AHEAD < packs:
                scores.append(score(pack + AHEAD))
            following = weigh(pack, scores[pack])
            if pack:
                add(pack - 1, *weighed)
            weighed = following
        add(packs - 1, *weighed)

    def one_run(part, carry):
        own = own_start(pos_ref, part)
        count = jnp.int32(0)
        for place, mask in enumerate(masks):
            for half in range(2):
                start = pos_ref[(me ^ mask) * (2 * SPAN) + half * SPAN]
                order[count] = place * 2 + half
                count = count + (start < own).astype(jnp.int32)
        odd = lax.rem(count, GROUP)
        for extra in range(last, GROUP):

            @pl.when(odd == extra)
            def _():
                slots = [order[place] for place in range(extra)]
                visit(part, slots if last else [part] + slots, not last)

        def several(step, carry):
            visit(part, [order[odd + GROUP * step + place] for place in range(GROUP)], False)
            return carry

        lax.fori_loop(0, lax.div(count, GROUP), several, 0)
        if last:
            rows = pl.ds(pl.multiple_of(part * SPAN, SPAN), SPAN)
            for head in range(heads):
                start = head % PACK * SPAN
                sums = total_ref[part, head // PACK, start : start + SPAN]
                out_ref[rows, head * HEAD_DIM : (head + 1) * HEAD_DIM] = (
                    sums[:, :HEAD_DIM] / sums[:, HEAD_DIM:]
                ).astype(out_ref.dtype)
        return carry

    lax.fori_loop(0, q_ref.shape[0] // SPAN, one_run, 0)


def attend(queries, pieces, positions, masks, state=()):
    last = bool(state)
    heads = queries.shape[1] // HEAD_DIM
    runs = queries.shape[0] // SPAN
    vmem = pl.BlockSpec(memory_space=pltpu.VMEM)
    smem = pl.BlockSpec(memory_space=pltpu.SMEM)
    shapes = [
        jax.ShapeDtypeStruct((runs, heads // PACK, PACK * SPAN, HEAD_DIM), jnp.float32),
        jax.ShapeDtypeStruct((runs, heads // PACK, PACK * SPAN, 2 * HEAD_DIM), jnp.float32),
    ]
    aliases = {}
    if last:
        shapes = [jax.ShapeDtypeStruct(queries.shape, jnp.bfloat16)] + shapes
        aliases = {3: 1, 4: 2}
    return pl.pallas_call(
        functools.partial(attention_kernel, masks, last),
        in_specs=[smem, vmem, vmem] + [vmem] * len(state),
        out_specs=[vmem] * len(shapes),
        out_shape=shapes,
        input_output_aliases=aliases,
        scratch_shapes=[pltpu.SMEM((2 * len(masks) + 1,), jnp.int32)],
        compiler_params=pltpu.CompilerParams(vmem_limit_bytes=24 * MIB),
    )(positions, queries, pieces, *state)


def exchanged(value, mask):
    count = lax.axis_size("outer") * lax.axis_size("inner")
    return lax.ppermute(value, SEQ_AXES, [(source, source ^ mask) for source in range(count)])


def body(tokens, positions, w_query, w_keyval):
    count = lax.axis_size("outer") * lax.axis_size("inner")
    masks = list(range(0, count, 2))
    stacked, turn = keyval(tokens, w_keyval, positions)
    direct = [stacked] + [exchanged(stacked, mask) for mask in masks[1:]]
    depths = (DEPTH,) * (tokens.shape[1] // DEPTH)
    queries = project(query_kernel, depths, [turn], tokens, w_query, [], [], 52)[0]
    queries, *direct = lax.optimization_barrier([queries, *direct])
    direct = jnp.concatenate(direct, 0)
    relayed = exchanged(direct, 1)
    state = attend(queries, direct, positions, masks)
    return attend(queries, relayed, positions, [mask ^ 1 for mask in masks], state)[0]


def solution(mesh):
    placed = (P(SEQ_AXES, None), P(), P(None, "head"), P(None, "head"))
    return jax.shard_map(
        body, mesh=mesh, in_specs=placed, out_specs=P(SEQ_AXES, "head"), check_vma=False
    )
```

profile of v0, /device:TPU:27, one launch (start us, length us, event | category | flops | bytes accessed | tf_op | source)
XLA Modules:
  0.0 43.2 jit_solution(6247970616194544798)
XLA Ops:
  0.0 7.2 %shard_map.64 = (bf16[512,256]{1,0:T(8,128)(2,1)}, f32[32768,128]{1,0:T(8,128)}) custom-call(s32[4096]{0:T(1024)} %pos_ref.3, f32[2,256,128]{2,1,0:T(8,128)} %constant.4.clone.within_hbm, f32[16,2,128]{2,1,0:T(2,128)} %constant.5.clone.starts_hbm, bf16[512,8192]{1,0:T(8,128)(2,1)} %tokens_hbm.3, bf16[8192,256]{1,0:T(8,128)(2,1)} %w_hbm.2), custom_call_target="tpu_custom_call" | custom-call | flops 2147483648 | bytes 12582912 | tf_op jit(solution)/shard_map/pallas_call | solution.py:166
  7.2 1.3 %collective-permute-start.2 = (bf16[512,256]{1,0:T(8,128)(2,1)}, bf16[512,256]{1,0:T(8,128)(2,1)S(1)}, u32[]{:S(2)}, u32[]{:S(2)}) collective-permute-start(bf16[512,256]{1,0:T(8,128)(2,1)} %get-tuple-element.18), channel_id=1, source_target_pairs={{0,6},{1,7},{2,4},{3,5},{4,2},{5,3},{6,0},{7,1},{8,14},{9,15},{10,... | collective-permute-start | bytes 786440 | tf_op jit(solution)/shard_map/ppermute | solution.py:348
  8.5 1.2 %collective-permute-start.1 = (bf16[512,256]{1,0:T(8,128)(2,1)}, bf16[512,256]{1,0:T(8,128)(2,1)S(1)}, u32[]{:S(2)}, u32[]{:S(2)}) collective-permute-start(bf16[512,256]{1,0:T(8,128)(2,1)} %get-tuple-element.18), channel_id=1, source_target_pairs={{0,4},{1,5},{2,6},{3,7},{4,0},{5,1},{6,2},{7,3},{8,12},{9,13},{10,... | collective-permute-start | bytes 786440 | tf_op jit(solution)/shard_map/ppermute | solution.py:348
  9.7 0.2 collective-permute-start
  9.9 0.0 copy-start.1
  9.9 0.0 copy-start
  9.9 11.6 %shard_map.65.q_ref = bf16[512,1024]{1,0:T(8,128)(2,1)S(1)} custom-call(f32[32768,128]{1,0:T(8,128)} %get-tuple-element.15.turn_hbm, bf16[512,8192]{1,0:T(8,128)(2,1)} %tokens_hbm.3, bf16[8192,1024]{1,0:T(8,128)(2,1)} %w_hbm.3), custom_call_target="tpu_custom_call" | custom-call | flops 8589934592 | bytes 25165824 | tf_op jit(solution)/shard_map/pallas_call | solution.py:166
  21.5 0.0 collective-permute-done.2
  21.5 0.0 collective-permute-done.1
  21.5 0.7 %collective-permute-done = bf16[512,256]{1,0:T(8,128)(2,1)S(1)} collective-permute-done((bf16[512,256]{1,0:T(8,128)(2,1)}, bf16[512,256]{1,0:T(8,128)(2,1)S(1)}, u32[]{:S(2)}, u32[]{:S(2)}) %collective-permute-start) | collective-permute-done | bytes 262176 | tf_op jit(solution)/shard_map/ppermute | solution.py:348
  22.2 0.0 copy-done.1
  22.3 0.9 %collective-permute-start.3 = (bf16[2048,256]{1,0:T(8,128)(2,1)S(1)}, bf16[2048,256]{1,0:T(8,128)(2,1)S(1)}, u32[]{:S(2)}, u32[]{:S(2)}) collective-permute-start(bf16[2048,256]{1,0:T(8,128)(2,1)S(1)} %constant_dynamic-update-slice_fusion.kv_ref), channel_id=1, source_target_pairs={{0,1},{1,0},{2,3},{3,2},{4,5},{5,4},{6,7},{7,6},{8,9},{9,8},{10,11... | collective-permute-start | bytes 3145736 | tf_op jit(solution)/shard_map/ppermute | solution.py:348
  23.2 0.0 copy-done
  23.2 9.1 %shard_map.66 = (f32[2,2,1024,128]{3,2,1,0:T(8,128)S(1)}, f32[2,2,1024,256]{3,2,1,0:T(8,128)S(1)}) custom-call(s32[4096]{0:T(1024)S(1)} %copy-done, bf16[512,1024]{1,0:T(8,128)(2,1)S(1)} %shard_map.65.q_ref, bf16[2048,256]{1,0:T(8,128)(2,1)S(1)} %constant_dynamic-update-slice_fusion.kv_ref), custom_call_target="tpu_custom_call" | custom-call | tf_op jit(solution)/shard_map/pallas_call | solution.py:335
  32.3 0.0 collective-permute-done.3.kv_ref
  32.3 10.9 %shard_map.67 = (bf16[512,1024]{1,0:T(8,128)(2,1)}, f32[2,2,1024,128]{3,2,1,0:T(8,128)S(1)}, f32[2,2,1024,256]{3,2,1,0:T(8,128)S(1)}) custom-call(s32[4096]{0:T(1024)S(1)} %copy-done, bf16[512,1024]{1,0:T(8,128)(2,1)S(1)} %shard_map.65.q_ref, bf16[2048,256]{1,0:T(8,128)(2,1)S(1)} %collective-permute-done.3.kv_ref, ...), custom_call_target="tpu_custom_call", output_to_operand_aliasing={{1}: (3, {}), {2}: (4, {})} | custom-call | tf_op jit(solution)/shard_map/pallas_call | solution.py:335
  (4 shorter events, 0.1 us)
Async XLA Ops:
  7.2 14.3 %collective-permute-start.2 = (bf16[512,256]{1,0:T(8,128)(2,1)}, bf16[512,256]{1,0:T(8,128)(2,1)S(1)}, u32[]{:S(2)}, u32[]{:S(2)}) collective-permute-start(bf16[512,256]{1,0:T(8,128)(2,1)} %get-tuple-element.18), channel_id=1, source_target_pairs={{0,6},{1,7},{2,4},{3,5},{4,2},{5,3},{6,0},{7,1},{8,14},{9,15},{10,... | collective-permute-start | bytes 786440 | tf_op jit(solution)/shard_map/ppermute | solution.py:348
  8.5 13.0 %collective-permute-start.1 = (bf16[512,256]{1,0:T(8,128)(2,1)}, bf16[512,256]{1,0:T(8,128)(2,1)S(1)}, u32[]{:S(2)}, u32[]{:S(2)}) collective-permute-start(bf16[512,256]{1,0:T(8,128)(2,1)} %get-tuple-element.18), channel_id=1, source_target_pairs={{0,4},{1,5},{2,6},{3,7},{4,0},{5,1},{6,2},{7,3},{8,12},{9,13},{10,... | collective-permute-start | bytes 786440 | tf_op jit(solution)/shard_map/ppermute | solution.py:348
  9.7 12.5 %collective-permute-start = (bf16[512,256]{1,0:T(8,128)(2,1)}, bf16[512,256]{1,0:T(8,128)(2,1)S(1)}, u32[]{:S(2)}, u32[]{:S(2)}) collective-permute-start(bf16[512,256]{1,0:T(8,128)(2,1)} %get-tuple-element.18), channel_id=1, source_target_pairs={{0,2},{1,3},{2,0},{3,1},{4,6},{5,7},{6,4},{7,5},{8,10},{9,11},{10,... | collective-permute-start | bytes 786440 | tf_op jit(solution)/shard_map/ppermute | solution.py:348
  9.9 12.3 %copy-start.1 = (bf16[512,256]{1,0:T(8,128)(2,1)S(1)}, bf16[512,256]{1,0:T(8,128)(2,1)}, u32[]{:S(2)}) copy-start(bf16[512,256]{1,0:T(8,128)(2,1)} %get-tuple-element.18) | copy-start | bytes 786436
  9.9 13.3 %copy-start = (s32[4096]{0:T(1024)S(1)}, s32[4096]{0:T(1024)}, u32[]{:S(2)}) copy-start(s32[4096]{0:T(1024)} %pos_ref.3) | copy-start | bytes 49156
  22.3 10.0 %collective-permute-start.3 = (bf16[2048,256]{1,0:T(8,128)(2,1)S(1)}, bf16[2048,256]{1,0:T(8,128)(2,1)S(1)}, u32[]{:S(2)}, u32[]{:S(2)}) collective-permute-start(bf16[2048,256]{1,0:T(8,128)(2,1)S(1)} %constant_dynamic-update-slice_fusion.kv_ref), channel_id=1, source_target_pairs={{0,1},{1,0},{2,3},{3,2},{4,5},{5,4},{6,7},{7,6},{8,9},{9,8},{10,11... | collective-permute-start | bytes 3145736 | tf_op jit(solution)/shard_map/ppermute | solution.py:348
where the time goes:
time: 44 us; the launch traced here: 43.2 us
  Pallas kernels  38.7 us (88%)
  starting transfers between devices  3.6 us (8%)
  waiting for transfers between devices  0.72 us (2%)
    pallas_call x2, Pallas kernels, attend(): pl.pallas_call(functools.partial(attention_kernel, masks, last), in_specs...  20 us
    pallas_call x2, Pallas kernels, project(): pl.pallas_call(functools.partial(kernel, depths), in_specs=[hbm] * (len(o...  18.7 us
    ppermute x4, starting transfers between devices, exchanged(): lax.ppermute(value, SEQ_AXES, [(source, source ^ mask) for source in rang...  3.6 us
  transfers between devices with their start and end apart: 4, of which 1 were waited for; matrix products, arithmetic and copies ran while one was open for 0% of the time, Pallas kernels for 48%

commit v1 on v0

--- a/solution.py
+++ b/solution.py
@@ -19,7 +19,7 @@
 BLOCK = 256
 DEPTH = 1024
 WINDOW = 3
-GROUP = 4
+GROUP = 5
 AHEAD = 1
 PACK = 4
 SEQ_AXES = ("outer", "inner")

time: 44 us -> 45.5 us (1.034)
  the two profiles are of different devices: /device:TPU:27 before, /device:TPU:30 now
where the time goes in v1:
time: 45.5 us; the launch traced here: 44.7 us
  Pallas kernels  40.9 us (90%)
  starting transfers between devices  3.62 us (8%)
    pallas_call x2, Pallas kernels, attend(): pl.pallas_call(functools.partial(attention_kernel, masks, last), in_specs...  22.1 us
    pallas_call x2, Pallas kernels, project(): pl.pallas_call(functools.partial(kernel, depths), in_specs=[hbm] * (len(o...  18.7 us
    ppermute x4, starting transfers between devices, exchanged(): lax.ppermute(value, SEQ_AXES, [(source, source ^ mask) for source in rang...  3.62 us
  transfers between devices with their start and end apart: 4, of which 0 were waited for; matrix products, arithmetic and copies ran while one was open for 0% of the time, Pallas kernels for 49%

profile of v1, /device:TPU:30, one launch (start us, length us, event | category | flops | bytes accessed | tf_op | source)
XLA Modules:
  0.0 44.7 jit_solution(15848973639363577621)
XLA Ops:
  0.0 7.2 %shard_map.64 = (bf16[512,256]{1,0:T(8,128)(2,1)}, f32[32768,128]{1,0:T(8,128)}) custom-call(s32[4096]{0:T(1024)} %pos_ref.3, f32[2,256,128]{2,1,0:T(8,128)} %constant.4.clone.within_hbm, f32[16,2,128]{2,1,0:T(2,128)} %constant.5.clone.starts_hbm, bf16[512,8192]{1,0:T(8,128)(2,1)} %tokens_hbm.3, bf16[8192,256]{1,0:T(8,128)(2,1)} %w_hbm.2), custom_call_target="tpu_custom_call" | custom-call | flops 2147483648 | bytes 12582912 | tf_op jit(solution)/shard_map/pallas_call | solution.py:166
  7.2 0.5 %collective-permute-start.2 = (bf16[512,256]{1,0:T(8,128)(2,1)}, bf16[512,256]{1,0:T(8,128)(2,1)S(1)}, u32[]{:S(2)}, u32[]{:S(2)}) collective-permute-start(bf16[512,256]{1,0:T(8,128)(2,1)} %get-tuple-element.18), channel_id=1, source_target_pairs={{0,6},{1,7},{2,4},{3,5},{4,2},{5,3},{6,0},{7,1},{8,14},{9,15},{10,... | collective-permute-start | bytes 786440 | tf_op jit(solution)/shard_map/ppermute | solution.py:348
  7.7 1.5 %collective-permute-start.1 = (bf16[512,256]{1,0:T(8,128)(2,1)}, bf16[512,256]{1,0:T(8,128)(2,1)S(1)}, u32[]{:S(2)}, u32[]{:S(2)}) collective-permute-start(bf16[512,256]{1,0:T(8,128)(2,1)} %get-tuple-element.18), channel_id=1, source_target_pairs={{0,4},{1,5},{2,6},{3,7},{4,0},{5,1},{6,2},{7,3},{8,12},{9,13},{10,... | collective-permute-start | bytes 786440 | tf_op jit(solution)/shard_map/ppermute | solution.py:348
  9.2 1.5 %collective-permute-start = (bf16[512,256]{1,0:T(8,128)(2,1)}, bf16[512,256]{1,0:T(8,128)(2,1)S(1)}, u32[]{:S(2)}, u32[]{:S(2)}) collective-permute-start(bf16[512,256]{1,0:T(8,128)(2,1)} %get-tuple-element.18), channel_id=1, source_target_pairs={{0,2},{1,3},{2,0},{3,1},{4,6},{5,7},{6,4},{7,5},{8,10},{9,11},{10,... | collective-permute-start | bytes 786440 | tf_op jit(solution)/shard_map/ppermute | solution.py:348
  10.7 0.0 copy-start.1
  10.8 0.0 copy-start
  10.8 11.6 %shard_map.65.q_ref = bf16[512,1024]{1,0:T(8,128)(2,1)S(1)} custom-call(f32[32768,128]{1,0:T(8,128)} %get-tuple-element.15.turn_hbm, bf16[512,8192]{1,0:T(8,128)(2,1)} %tokens_hbm.3, bf16[8192,1024]{1,0:T(8,128)(2,1)} %w_hbm.3), custom_call_target="tpu_custom_call" | custom-call | flops 8589934592 | bytes 25165824 | tf_op jit(solution)/shard_map/pallas_call | solution.py:166
  22.3 0.0 collective-permute-done.2
  22.3 0.0 collective-permute-done.1
  22.3 0.0 collective-permute-done
  22.4 0.0 copy-done.1
  22.5 0.1 collective-permute-start.3
  22.5 0.0 copy-done
  22.6 10.4 %shard_map.66 = (f32[2,2,1024,128]{3,2,1,0:T(8,128)S(1)}, f32[2,2,1024,256]{3,2,1,0:T(8,128)S(1)}) custom-call(s32[4096]{0:T(1024)S(1)} %copy-done, bf16[512,1024]{1,0:T(8,128)(2,1)S(1)} %shard_map.65.q_ref, bf16[2048,256]{1,0:T(8,128)(2,1)S(1)} %constant_dynamic-update-slice_fusion.kv_ref), custom_call_target="tpu_custom_call" | custom-call | tf_op jit(solution)/shard_map/pallas_call | solution.py:335
  33.0 0.0 collective-permute-done.3.kv_ref
  33.0 11.7 %shard_map.67 = (bf16[512,1024]{1,0:T(8,128)(2,1)}, f32[2,2,1024,128]{3,2,1,0:T(8,128)S(1)}, f32[2,2,1024,256]{3,2,1,0:T(8,128)S(1)}) custom-call(s32[4096]{0:T(1024)S(1)} %copy-done, bf16[512,1024]{1,0:T(8,128)(2,1)S(1)} %shard_map.65.q_ref, bf16[2048,256]{1,0:T(8,128)(2,1)S(1)} %collective-permute-done.3.kv_ref, ...), custom_call_target="tpu_custom_call", output_to_operand_aliasing={{1}: (3, {}), {2}: (4, {})} | custom-call | tf_op jit(solution)/shard_map/pallas_call | solution.py:335
  (4 shorter events, 0.1 us)
Async XLA Ops:
  7.2 15.1 %collective-permute-start.2 = (bf16[512,256]{1,0:T(8,128)(2,1)}, bf16[512,256]{1,0:T(8,128)(2,1)S(1)}, u32[]{:S(2)}, u32[]{:S(2)}) collective-permute-start(bf16[512,256]{1,0:T(8,128)(2,1)} %get-tuple-element.18), channel_id=1, source_target_pairs={{0,6},{1,7},{2,4},{3,5},{4,2},{5,3},{6,0},{7,1},{8,14},{9,15},{10,... | collective-permute-start | bytes 786440 | tf_op jit(solution)/shard_map/ppermute | solution.py:348
  7.7 14.6 %collective-permute-start.1 = (bf16[512,256]{1,0:T(8,128)(2,1)}, bf16[512,256]{1,0:T(8,128)(2,1)S(1)}, u32[]{:S(2)}, u32[]{:S(2)}) collective-permute-start(bf16[512,256]{1,0:T(8,128)(2,1)} %get-tuple-element.18), channel_id=1, source_target_pairs={{0,4},{1,5},{2,6},{3,7},{4,0},{5,1},{6,2},{7,3},{8,12},{9,13},{10,... | collective-permute-start | bytes 786440 | tf_op jit(solution)/shard_map/ppermute | solution.py:348
  9.2 13.1 %collective-permute-start = (bf16[512,256]{1,0:T(8,128)(2,1)}, bf16[512,256]{1,0:T(8,128)(2,1)S(1)}, u32[]{:S(2)}, u32[]{:S(2)}) collective-permute-start(bf16[512,256]{1,0:T(8,128)(2,1)} %get-tuple-element.18), channel_id=1, source_target_pairs={{0,2},{1,3},{2,0},{3,1},{4,6},{5,7},{6,4},{7,5},{8,10},{9,11},{10,... | collective-permute-start | bytes 786440 | tf_op jit(solution)/shard_map/ppermute | solution.py:348
  10.7 11.6 %copy-start.1 = (bf16[512,256]{1,0:T(8,128)(2,1)S(1)}, bf16[512,256]{1,0:T(8,128)(2,1)}, u32[]{:S(2)}) copy-start(bf16[512,256]{1,0:T(8,128)(2,1)} %get-tuple-element.18) | copy-start | bytes 786436
  10.8 11.8 %copy-start = (s32[4096]{0:T(1024)S(1)}, s32[4096]{0:T(1024)}, u32[]{:S(2)}) copy-start(s32[4096]{0:T(1024)} %pos_ref.3) | copy-start | bytes 49156
  22.5 10.5 %collective-permute-start.3 = (bf16[2048,256]{1,0:T(8,128)(2,1)S(1)}, bf16[2048,256]{1,0:T(8,128)(2,1)S(1)}, u32[]{:S(2)}, u32[]{:S(2)}) collective-permute-start(bf16[2048,256]{1,0:T(8,128)(2,1)S(1)} %constant_dynamic-update-slice_fusion.kv_ref), channel_id=1, source_target_pairs={{0,1},{1,0},{2,3},{3,2},{4,5},{5,4},{6,7},{7,6},{8,9},{9,8},{10,11... | collective-permute-start | bytes 3145736 | tf_op jit(solution)/shard_map/ppermute | solution.py:348
